TPU v7x, 32 devices: a whole 2x2x4 slice. The times are simulated.
32 devices in a mesh: rep: 16 (over z, y, core), shard: 2 (over x).
Axes of the slice: x: 2, y: 2, z: 4, core: 2. Of those that a mesh axis runs over, the one named last changes fastest.
Arguments:
- tokens: bfloat16 [4096, 2048], P(('rep', 'shard')), may hold values from -6 to 6
- routes: int32 [4096, 2], P(('rep', 'shard')), may hold values from 0 to 7, all different within a row; in each aligned block of 128 rows (0 to 127, 128 to 255, ...) at most 48 rows name the same one
- route_weight: float32 [4096, 2], P(('rep', 'shard')), may hold values from 0.2 to 1
- w_gate: bfloat16 [8, 2048, 768], P('shard'), may hold values from -0.125 to 0.125
- w_up: bfloat16 [8, 2048, 768], P('shard'), may hold values from -0.125 to 0.125
- w_down: bfloat16 [8, 768, 2048], P('shard'), may hold values from -0.21875 to 0.21875
- pseudo_grad: float32 [16, 192, 2048], P('rep', 'shard'), may hold values from -5400 to 5400
- global_params: float32 [192, 2048], P('shard'), may hold values from -6 to 6
- momentum: float32 [192, 2048], P('shard', 'rep'), may hold values from -3 to 3
- local_params: bfloat16 [16, 192, 2048], P('rep', 'shard'), may hold values from -6 to 6
Outputs:
- moe_out: bfloat16 [4096, 2048], P(('rep', 'shard'))
- momentum_next: float32 [192, 2048], P('shard', 'rep')
- local_next: bfloat16 [16, 192, 2048], P('rep', 'shard')
Inputs may be any that keep to these rules, and one draw needn't show every extreme that they name: `routes`: each token names 2 different experts. Within the rows of one device no expert is named by more than 48 rows, and on some device one is named by exactly 48.
All inputs are finite; a program needn't handle non-finite values.
Results may differ from a plain program's by a relative error of at most 0.0057.
Values may be sent and summed in bfloat16 or wider, within the bound.
A program may use at most 128 MiB of HBM per device.

v0:
```python
import jax
import jax.numpy as jnp
from jax import lax
from jax.sharding import PartitionSpec as P

outer_momentum = 0.9
outer_rate = 0.7
merge_weight = 0.5
clip_epsilon = 1e-06


def slot_table(flat_routes, experts, capacity):
    one_hot = (flat_routes[:, None] == jnp.arange(experts, dtype=jnp.int32)[None, :]).astype(
        jnp.int32
    )
    earlier = jnp.cumsum(one_hot, axis=0) - one_hot
    position = jnp.sum(earlier * one_hot, axis=1)
    return flat_routes * capacity + position


def local(
    tokens,
    routes,
    route_weight,
    w_gate,
    w_up,
    w_down,
    pseudo_grad,
    global_params,
    momentum,
    local_params,
):
    tok_rows, feat_width = tokens.shape
    top_count = routes.shape[1]
    local_experts = w_gate.shape[0]
    experts = local_experts * lax.axis_size("shard")
    capacity = tok_rows * 3 // 8
    slot_index = slot_table(routes.reshape(-1), experts, capacity)
    matches = (
        jnp.arange(experts * capacity, dtype=jnp.int32)[:, None] == slot_index[None, :]
    ).astype(jnp.bfloat16)
    placement = jnp.sum(matches.reshape(experts * capacity, tok_rows, top_count), axis=2)
    outgoing = jnp.dot(placement, tokens, preferred_element_type=jnp.float32).astype(jnp.bfloat16)
    outgoing = outgoing.reshape(experts, capacity, feat_width)
    received = lax.all_to_all(outgoing, "shard", split_axis=0, concat_axis=0, tiled=True)
    total_rows = received.shape[0]
    slot_count = received.shape[1]
    grouped = received.reshape(total_rows // local_experts, local_experts, slot_count, feat_width)
    gate = jnp.einsum("spcd,pdf->spcf", grouped, w_gate, preferred_element_type=jnp.float32)
    upward = jnp.einsum("spcd,pdf->spcf", grouped, w_up, preferred_element_type=jnp.float32)
    hidden = (jax.nn.silu(gate) * upward).astype(jnp.bfloat16)
    result = jnp.einsum(
        "spcf,pfd->spcd", hidden, w_down, preferred_element_type=jnp.float32
    ).astype(jnp.bfloat16)
    result = result.reshape(total_rows, slot_count, feat_width)
    returned = lax.all_to_all(result, "shard", split_axis=0, concat_axis=0, tiled=True)
    picked = returned.reshape(experts * capacity, feat_width)[slot_index]
    picked = picked.reshape(tok_rows, top_count, feat_width).astype(jnp.float32)
    moe_out = jnp.sum(route_weight[:, :, None] * picked, axis=1).astype(jnp.bfloat16)
    replicas = lax.axis_size("rep")
    own_delta = pseudo_grad[0]
    frag_rows = own_delta.shape[0]
    entry_count = float(frag_rows * lax.axis_size("shard") * feat_width)
    col_width = momentum.shape[1]
    col_start = lax.axis_index("rep") * col_width
    delta_total = lax.psum(own_delta, "rep")
    mean_delta = delta_total / replicas
    square_sum = lax.psum(jnp.sum(mean_delta * mean_delta), "shard")
    clip_factor = jnp.minimum(1.0, lax.rsqrt(square_sum / entry_count + clip_epsilon))
    clipped = clip_factor * mean_delta
    full_momentum = lax.all_gather(momentum, "rep", axis=1, tiled=True)
    momentum_full = outer_momentum * full_momentum + clipped
    global_next = global_params - outer_rate * (outer_momentum * momentum_full + clipped)
    momentum_next = lax.dynamic_slice_in_dim(momentum_full, col_start, col_width, 1)
    local_next = (
        merge_weight * local_params.astype(jnp.float32) + (1.0 - merge_weight) * global_next[None]
    ).astype(jnp.bfloat16)
    return (moe_out, momentum_next, local_next)


def solution(mesh):
    in_specs = (
        P(("rep", "shard"), None),
        P(("rep", "shard"), None),
        P(("rep", "shard"), None),
        P("shard", None, None),
        P("shard", None, None),
        P("shard", None, None),
        P("rep", "shard", None),
        P("shard", None),
        P("shard", "rep"),
        P("rep", "shard", None),
    )
    out_specs = (P(("rep", "shard"), None), P("shard", "rep"), P("rep", "shard", None))
    return jax.shard_map(local, mesh=mesh, in_specs=in_specs, out_specs=out_specs, check_vma=False)
```

profile of v0, /device:TPU:0, one launch (start us, length us, event | category | flops | bytes accessed | tf_op | source)
XLA Modules:
  0.0 183.2 jit_solution(16061809618244788950)
XLA Ops:
  7.2 0.0 copy-start
  7.2 0.8 copy.22
  8.0 0.1 eq.44
  8.2 0.1 eq.40
  8.3 0.6 reduce-window.6
  8.9 0.2 slice_reduce_fusion
  9.2 0.1 fusion.44
  9.3 0.1 reduce_sum.44
  9.4 0.1 copy.25
  9.5 0.1 fusion.42
  9.6 0.0 copy-done
  9.6 1.7 convolution_convert_fusion
  11.3 0.0 copy-start.6
  11.3 0.0 copy-start.5
  11.3 4.3 %all-to-all-start = ((bf16[8,48,2048]{2,1,0:T(8,128)(2,1)}), bf16[8,48,2048]{2,1,0:T(8,128)(2,1)S(1)}, u32[]{:S(2)}, u32[]{:S(2)}) async-start(bf16[8,48,2048]{2,1,0:T(8,128)(2,1)} %bitcast.67), calls=%async_computation | async-start | bytes 3145728 | tf_op jit(solution)/shard_map/all_to_all | solution.py:45
  15.6 0.0 all-reduce.2.cloned.1.call-start
  15.6 0.7 all-reduce.2.cloned.1.call-update
  16.3 0.1 mul.74
  16.5 0.0 copy-done.6
  16.5 0.1 copy.21
  16.6 0.0 copy-done.5
  16.6 26.8 %all_gather.3 = f32[96,2048]{1,0:T(8,128)} all-gather(f32[96,128]{1,0:T(8,128)S(1)} %copy-done.5), channel_id=1, replica_groups=mesh['rep'=16,'shard'=2] {'rep'}, dimensions={1}, use_global_device_ids=true | all-gather | bytes 835584 | tf_op jit(solution)/shard_map/all_gather | solution.py:71
  43.4 72.0 %all-reduce.2.cloned.1.call-done = f32[96,2048]{1,0:T(8,128)} async-done(((f32[96,2048]{1,0:T(8,128)}), f32[96,2048]{1,0:T(8,128)}) %all-reduce.2.cloned.1.call-update) | async-done | bytes 786448 | tf_op jit(solution)/shard_map/psum | solution.py:66
  115.4 1.9 %multiply_reduce_fusion.1 = f32[]{:T(128)} fusion(f32[96,2048]{1,0:T(8,128)} %all-reduce.2.cloned.1.call-done), kind=kLoop, calls=%fused_computation.24 | loop fusion | flops 589823 | bytes 786436 | tf_op jit(solution)/shard_map/reduce_sum | solution.py:68
  117.3 5.5 %psum.15 = f32[]{:T(128)} all-reduce(f32[]{:T(128)} %multiply_reduce_fusion.1), channel_id=1, replica_groups=mesh['rep'=16,'shard'=2] {'shard'}, use_global_device_ids=true, to_apply=%region_7.8 | all-reduce | flops 1 | bytes 8 | tf_op jit(solution)/shard_map/psum | solution.py:68
  123.6 0.0 all-to-all-done
  123.6 6.6 %fusion.12 = f32[2,4,48,768]{3,2,0,1:T(8,128)S(1)} fusion(bf16[4,2048,768]{2,1,0:T(8,128)(2,1)} %param.13, bf16[2,4,48,2048]{3,2,1,0:T(8,128)(2,1)S(1)} %bitcast.65), kind=kOutput, calls=%fused_computation.11 | convolution fusion | flops 1207959552 | bytes 15335424 | tf_op jit(solution)/shard_map/spcd,pdf->spcf/dot_general | solution.py:49
  130.1 13.5 %fusion.9 = bf16[2,4,48,2048]{3,2,0,1:T(8,128)(2,1)} fusion(bf16[4,768,2048]{2,1,0:T(8,128)(2,1)} %param.15, bf16[4,2048,768]{2,1,0:T(8,128)(2,1)} %param.14, bf16[2,4,48,2048]{3,2,1,0:T(8,128)(2,1)S(1)} %bitcast.66, f32[2,4,48,768]{3,2,0,1:T(8,128)S(1)} %fusion.12), kind=kOutput, calls=%fused_computation.9 | convolution fusion | flops 2418475008 | bytes 29491200 | tf_op jit(solution)/shard_map/spcf,pfd->spcd/dot_general | solution.py:52
  143.7 2.7 %copy.28 = bf16[2,4,48,2048]{3,2,1,0:T(8,128)(2,1)} copy(bf16[2,4,48,2048]{3,2,0,1:T(8,128)(2,1)} %fusion.9) | data formatting | bytes 3145728 | tf_op jit(solution)/shard_map/convert_element_type | solution.py:54
  146.4 0.0 copy-start.1
  146.4 4.0 %all-to-all-start.1 = ((bf16[8,48,2048]{2,1,0:T(8,128)(2,1)}), bf16[8,48,2048]{2,1,0:T(8,128)(2,1)S(1)}, u32[]{:S(2)}, u32[]{:S(2)}) async-start(bf16[8,48,2048]{2,1,0:T(8,128)(2,1)} %bitcast.68), calls=%async_computation.1 | async-start | bytes 3145728 | tf_op jit(solution)/shard_map/all_to_all | solution.py:56
  150.4 0.0 copy-done.1
  150.4 0.0 copy-start.2
  150.4 0.0 copy-start.3
  150.4 0.0 copy-start.4
  150.4 1.4 multiply_add_fusion
  151.8 0.6 constant_dynamic-slice_fusion
  152.4 0.0 copy-done.2
  152.4 0.0 copy-done.3
  152.4 0.0 copy-done.4
  152.4 1.0 fusion.39
  153.5 14.2 %all-to-all-done.1 = bf16[8,48,2048]{2,1,0:T(8,128)(2,1)S(1)} async-done(((bf16[8,48,2048]{2,1,0:T(8,128)(2,1)}), bf16[8,48,2048]{2,1,0:T(8,128)(2,1)S(1)}, u32[]{:S(2)}, u32[]{:S(2)}) %all-to-all-start.1) | async-done | bytes 1572896 | tf_op jit(solution)/shard_map/all_to_all | solution.py:56
  167.7 2.3 %gather_fusion = bf16[256,2048]{1,0:T(8,128)(2,1)} fusion(bf16[384,2048]{1,0:T(8,128)(2,1)S(1)} %bitcast.64, s32[1024]{0:T(1024)S(1)} %pad_clamp_fusion), kind=kCustom, calls=%fused_computation | custom fusion | bytes 2098176 | tf_op jit(solution)/shard_map/gather | solution.py:57
  170.0 2.4 %reshape.90 = f32[128,2,2048]{2,1,0:T(2,128)S(1)} reshape(bf16[256,2048]{1,0:T(8,128)(2,1)} %gather_fusion) | data formatting | bytes 3145728 | tf_op jit(solution)/shard_map/convert_element_type | solution.py:58
  172.4 3.9 %multiply_reduce_fusion = bf16[128,2048]{1,0:T(8,128)(2,1)} fusion(f32[128,2,2048]{2,1,0:T(2,128)S(1)} %reshape.90, f32[128,2]{1,0:T(8,128)S(1)} %copy.21), kind=kLoop, calls=%fused_computation.10 | loop fusion | flops 786432 | bytes 2622464 | tf_op jit(solution)/shard_map/reduce_sum | solution.py:59
  (6 shorter events, 0.1 us)
Async XLA Ops:
  7.2 2.4 %copy-start = (bf16[128,2048]{1,0:T(8,128)(2,1)S(1)}, bf16[128,2048]{1,0:T(8,128)(2,1)}, u32[]{:S(2)}) copy-start(bf16[128,2048]{1,0:T(8,128)(2,1)} %param.10) | copy-start | bytes 1572868
  11.3 5.2 %copy-start.6 = (f32[128,2]{0,1:T(2,128)S(1)}, f32[128,2]{0,1:T(2,128)}, u32[]{:S(2)}) copy-start(f32[128,2]{0,1:T(2,128)} %param.12) | copy-start | bytes 3076
  11.3 5.4 %copy-start.5 = (f32[96,128]{1,0:T(8,128)S(1)}, f32[96,128]{1,0:T(8,128)}, u32[]{:S(2)}) copy-start(f32[96,128]{1,0:T(8,128)} %param.18) | copy-start | bytes 147460
  11.3 112.3 %all-to-all-start = ((bf16[8,48,2048]{2,1,0:T(8,128)(2,1)}), bf16[8,48,2048]{2,1,0:T(8,128)(2,1)S(1)}, u32[]{:S(2)}, u32[]{:S(2)}) async-start(bf16[8,48,2048]{2,1,0:T(8,128)(2,1)} %bitcast.67), calls=%async_computation | async-start | bytes 3145728 | tf_op jit(solution)/shard_map/all_to_all | solution.py:45
  15.6 99.7 %all-reduce.2.cloned.1.call-start = ((), (), s32[]{:S(2)}) async-start(), calls=%async_computation.2 | async-start | bytes 1572864 | tf_op jit(solution)/shard_map/psum | solution.py:66
  146.4 4.0 %copy-start.1 = (f32[96,2048]{1,0:T(8,128)S(1)}, f32[96,2048]{1,0:T(8,128)}, u32[]{:S(2)}) copy-start(f32[96,2048]{1,0:T(8,128)} %all-reduce.2.cloned.1.call-done) | copy-start | bytes 2359300
  146.4 21.3 %all-to-all-start.1 = ((bf16[8,48,2048]{2,1,0:T(8,128)(2,1)}), bf16[8,48,2048]{2,1,0:T(8,128)(2,1)S(1)}, u32[]{:S(2)}, u32[]{:S(2)}) async-start(bf16[8,48,2048]{2,1,0:T(8,128)(2,1)} %bitcast.68), calls=%async_computation.1 | async-start | bytes 3145728 | tf_op jit(solution)/shard_map/all_to_all | solution.py:56
  150.4 2.0 %copy-start.2 = (f32[96,2048]{1,0:T(8,128)S(1)}, f32[96,2048]{1,0:T(8,128)}, u32[]{:S(2)}) copy-start(f32[96,2048]{1,0:T(8,128)} %all_gather.3) | copy-start | bytes 2359300
  150.4 2.0 %copy-start.3 = (f32[96,2048]{1,0:T(8,128)S(1)}, f32[96,2048]{1,0:T(8,128)}, u32[]{:S(2)}) copy-start(f32[96,2048]{1,0:T(8,128)} %param.17) | copy-start | bytes 2359300
  150.4 2.0 %copy-start.4 = (bf16[1,96,2048]{2,1,0:T(8,128)(2,1)S(1)}, bf16[1,96,2048]{2,1,0:T(8,128)(2,1)}, u32[]{:S(2)}) copy-start(bf16[1,96,2048]{2,1,0:T(8,128)(2,1)} %param.19) | copy-start | bytes 1179652
Sparse Core Ops, SparseCore 0:
  19.8 95.4 all-reduce.1
where the time goes:
time: 184 us; the launch traced here: 183 us
  waiting for transfers between devices  86.9 us (47%)
  blocking collectives  32.3 us (18%)
  matrix products  21.8 us (12%)
  between operations  14.9 us (8%)
  local copies, waits for them, and re-layouts  9.91 us (5%)
  other arithmetic  9.08 us (5%)
  starting transfers between devices  8.32 us (5%)
    psum x1, waiting for transfers between devices, local(): delta_total = lax.psum(own_delta, 'rep')  72 us
    all_gather x1, blocking collectives, local(): full_momentum = lax.all_gather(momentum, 'rep', axis=1, tiled=True)  26.8 us
    all_to_all x1, waiting for transfers between devices, local(): lax.all_to_all(result, 'shard', split_axis=0, concat_axis=0, tiled=True)  14.2 us
    dot_general x1, matrix products, local(): jnp.einsum('spcf,pfd->spcd', hidden, w_down, preferred_element_type=jnp.f...  13.5 us
    dot_general x1, matrix products, local(): jnp.einsum('spcd,pdf->spcf', grouped, w_gate, preferred_element_type=jnp....  6.56 us
    psum x1, blocking collectives, local(): square_sum = lax.psum(jnp.sum(mean_delta * mean_delta), 'shard')  5.55 us
    all_to_all x1, starting transfers between devices, local(): lax.all_to_all(outgoing, 'shard', split_axis=0, concat_axis=0, tiled=True)  4.34 us
    all_to_all x1, starting transfers between devices, local(): lax.all_to_all(result, 'shard', split_axis=0, concat_axis=0, tiled=True)  3.98 us
  transfers between devices with their start and end apart: 3, of which 2 were waited for; matrix products, arithmetic and copies ran while one was open for 3% of the time, Pallas kernels for 0%

commit v1 on v0

--- a/solution.py
+++ b/solution.py
@@ -1,6 +1,10 @@
+import functools
+
 import jax
 import jax.numpy as jnp
 from jax import lax
+from jax.experimental import pallas as pl
+from jax.experimental.pallas import tpu as pltpu
 from jax.sharding import PartitionSpec as P
 
 outer_momentum = 0.9
@@ -78,6 +82,437 @@
     return (moe_out, momentum_next, local_next)
 
 
+LANES = 128
+MESH = pl.DeviceIdType.MESH
+
+
+def kernel(
+    reps,
+    tokens,
+    routes,
+    route_weight,
+    w_gate,
+    w_up,
+    w_down,
+    pseudo_grad,
+    global_params,
+    momentum,
+    local_params,
+    moe_out,
+    momentum_next,
+    local_next,
+    gate_s,
+    up_s,
+    down_s,
+    own_tok,
+    far_tok,
+    mix_own,
+    mix_send,
+    mix_far,
+    col_own,
+    col_far,
+    hid_own,
+    hid_far,
+    sum_own,
+    back_send,
+    back,
+    out_s,
+    grad_own,
+    grad_sib,
+    grad_sum,
+    grad_far,
+    sq_own,
+    sq_far,
+    sq_chip,
+    sq_sib,
+    sq_half,
+    sq_other,
+    mom_s,
+    glob_s,
+    loc_s,
+    upd,
+    mom_out,
+    loc_out,
+    w_sem,
+    in_sem,
+    out_sem,
+    g_sem,
+    tok_sem,
+    mix_sem,
+    back_sem,
+    sib_sem,
+    far_sem,
+    sq_sem,
+    one_sem,
+    upd_sem,
+    fwd_sem,
+):
+    experts = w_gate.shape[0]
+    rows, width = tokens.shape
+    hidden = w_gate.shape[2]
+    chunks, tiles, chunk_rows, tile_cols = back.shape
+    frag_rows = momentum.shape[0]
+    chips = reps // 2
+
+    rep = lax.axis_index("rep")
+    shard = lax.axis_index("shard")
+    chip = rep // 2
+    core = rep % 2
+    partner = (rep, 1 - shard)
+    sibling = (chip * 2 + 1 - core, shard)
+
+    def peer(step):
+        return (((chip + step) % chips) * 2 + core, shard)
+
+    def columns(index):
+        return pl.ds(pl.multiple_of(index * LANES, LANES), LANES)
+
+    weights = []
+    for e in range(experts):
+        weights.append(pltpu.make_async_copy(w_gate.at[e], gate_s.at[e], w_sem.at[0, e]))
+        weights.append(pltpu.make_async_copy(w_up.at[e], up_s.at[e], w_sem.at[1, e]))
+    for e in range(experts):
+        weights.append(
+            pltpu.make_async_copy(w_down.at[e], down_s.at[pl.ds(e * hidden, hidden)], w_sem.at[2, e])
+        )
+    load_tok = pltpu.make_async_copy(tokens, own_tok, in_sem.at[0])
+    load_glob = pltpu.make_async_copy(global_params, glob_s, in_sem.at[1])
+    load_mom = pltpu.make_async_copy(momentum, mom_s, in_sem.at[2])
+    load_loc = pltpu.make_async_copy(local_params.at[0], loc_s, in_sem.at[3])
+    load_grad = [
+        pltpu.make_async_copy(
+            pseudo_grad.at[0, :, columns(2 * k + core)], grad_own.at[k], g_sem.at[k]
+        )
+        for k in range(chips)
+    ]
+
+    load_tok.start()
+    for copy in weights[:2]:
+        copy.start()
+    for copy in load_grad:
+        copy.start()
+
+    ids = lax.broadcasted_iota(jnp.int32, (8, rows), 0)
+    mix = jnp.zeros((8, rows), jnp.float32)
+    for k in range(routes.shape[0]):
+        mix = mix + jnp.where(ids == routes[k : k + 1, :], route_weight[k : k + 1, :], 0.0)
+    mix_send[...] = mix
+    rest = jnp.zeros((LANES - 8, rows), jnp.float32)
+    mix_own[...] = jnp.concatenate([mix, rest], axis=0).T
+
+    barrier = pltpu.get_barrier_semaphore()
+    for device in [partner, sibling] + [peer(j) for j in range(1, chips)]:
+        pl.semaphore_signal(barrier, inc=1, device_id=device, device_id_type=MESH)
+    pl.semaphore_wait(barrier, 1 + chips)
+
+    def remote(src, dst, sems, index, device):
+        return pltpu.make_async_remote_copy(
+            src_ref=src,
+            dst_ref=dst,
+            send_sem=sems.at[(0,) + index],
+            recv_sem=sems.at[(1,) + index],
+            device_id=device,
+            device_id_type=MESH,
+        )
+
+    send_mix = remote(mix_send, mix_far, mix_sem, (0,), partner)
+    send_mix.start()
+    send_tok = []
+    for c in range(chunks):
+        part = pl.ds(c * chunk_rows, chunk_rows)
+        send_tok.append(remote(tokens.at[part], far_tok.at[part], tok_sem, (c,), partner))
+        send_tok[c].start()
+    send_sib = []
+    for k in range(chips):
+        send_sib.append(
+            remote(
+                pseudo_grad.at[0, :, columns(2 * k + 1 - core)], grad_sib.at[k], sib_sem, (k,), sibling
+            )
+        )
+        send_sib[k].start()
+    for copy in weights[2:]:
+        copy.start()
+    load_loc.start()
+    load_glob.start()
+    load_mom.start()
+
+    def gate_up(tok, part, col, hid, e):
+        tok_part = tok[part, :]
+        scale = col[part, pl.ds(0, 1)]
+        for f in range(0, hidden, 256):
+            gate = jnp.dot(tok_part, gate_s[e, :, f : f + 256], preferred_element_type=jnp.float32)
+            upward = jnp.dot(tok_part, up_s[e, :, f : f + 256], preferred_element_type=jnp.float32)
+            value = gate / (1.0 + jnp.exp(-gate)) * upward * scale
+            hid[part, pl.ds(pl.multiple_of(e * hidden + f, LANES), 256)] = value.astype(jnp.bfloat16)
+
+    def pick(mix_ref, col, e):
+        lanes = lax.broadcasted_iota(jnp.int32, (rows, LANES), 1)
+        chosen = jnp.where(lanes == shard * experts + e, mix_ref[...], 0.0)
+        col[...] = jnp.broadcast_to(jnp.sum(chosen, axis=1, keepdims=True), (rows, LANES))
+
+    whole = pl.ds(0, rows)
+
+    def own_step(e, carry):
+        pltpu.make_async_copy(w_gate.at[e], gate_s.at[e], w_sem.at[0, e]).wait()
+        pltpu.make_async_copy(w_up.at[e], up_s.at[e], w_sem.at[1, e]).wait()
+        pick(mix_own, col_own, e)
+        gate_up(own_tok, whole, col_own, hid_own, e)
+        return carry
+
+    load_tok.wait()
+    lax.fori_loop(0, experts // 2, own_step, 0)
+
+    for copy in load_grad:
+        copy.wait()
+    for copy in send_sib:
+        copy.wait_recv()
+
+    def chip_sum(k, carry):
+        grad_sum[k] = grad_own[k] + grad_sib[k]
+        return carry
+
+    lax.fori_loop(0, chips, chip_sum, 0)
+    send_far = []
+    for j in range(1, chips):
+        send_far.append(
+            remote(grad_sum.at[(chip + j) % chips], grad_far.at[j - 1], far_sem, (j - 1,), peer(j))
+        )
+        send_far[j - 1].start()
+
+    lax.fori_loop(experts // 2, experts, own_step, 0)
+
+    send_mix.wait_recv()
+    mix_own[...] = jnp.concatenate([mix_far[...], rest], axis=0).T
+
+    def far_rows(c):
+        part = pl.ds(c * chunk_rows, chunk_rows)
+        send_tok[c].wait_recv()
+
+        def far_step(e, carry):
+            pick(mix_own, col_far, e)
+            gate_up(far_tok, part, col_far, hid_far, e)
+            return carry
+
+        lax.fori_loop(0, experts, far_step, 0)
+
+    def down(hid_part, t):
+        return jnp.dot(
+            hid_part,
+            down_s[:, t * tile_cols : (t + 1) * tile_cols],
+            preferred_element_type=jnp.float32,
+        )
+
+    send_back = []
+
+    def far_down(c):
+        part = pl.ds(c * chunk_rows, chunk_rows)
+        for t in range(tiles):
+            back_send[c, t] = down(hid_far[part, :], t).astype(jnp.bfloat16)
+            copy = remote(back_send.at[c, t], back.at[c, t], back_sem, (c, t), partner)
+            copy.start()
+            send_back.append(copy)
+
+    far_rows(0)
+    for copy in weights[2 * experts :]:
+        copy.wait()
+    far_down(0)
+    for c in range(1, chunks):
+        far_rows(c)
+        far_down(c)
+
+    for copy in send_far:
+        copy.wait_recv()
+    total = grad_sum[chip]
+    for j in range(1, chips):
+        total = total + grad_far[j - 1]
+    mean = total / reps
+    squares = mean * mean
+    square = squares[0:8]
+    for i in range(8, frag_rows, 8):
+        square = square + squares[i : i + 8]
+    sq_own[...] = square
+    send_sq = []
+    for j in range(1, chips):
+        send_sq.append(remote(sq_own, sq_far.at[j - 1], sq_sem, (j - 1,), peer(j)))
+        send_sq[j - 1].start()
+
+    for t in range(tiles):
+        sum_own[:, t * tile_cols : (t + 1) * tile_cols] = down(hid_own[...], t)
+
+    for copy in send_sq:
+        copy.wait_recv()
+    square = sq_own[...]
+    for j in range(1, chips):
+        square = square + sq_far[j - 1]
+    sq_chip[...] = square
+    to_sib = remote(sq_chip, sq_sib, one_sem, (0,), sibling)
+    to_sib.start()
+    to_sib.wait_recv()
+    sq_half[...] = sq_chip[...] + sq_sib[...]
+    to_other = remote(sq_half, sq_other, one_sem, (1,), partner)
+    to_other.start()
+    to_other.wait_recv()
+    entries = float(frag_rows * 2 * width)
+    square_sum = jnp.sum(sq_half[...] + sq_other[...])
+    clip_factor = jnp.minimum(1.0, lax.rsqrt(square_sum / entries + clip_epsilon))
+    clipped = clip_factor * mean
+    load_mom.wait()
+    fresh = outer_momentum * mom_s[...] + clipped
+    mom_out[...] = fresh
+    store_mom = pltpu.make_async_copy(mom_out, momentum_next, out_sem.at[0])
+    store_mom.start()
+    upd[rep] = (outer_rate * (outer_momentum * fresh + clipped)).astype(jnp.bfloat16)
+
+    send_upd = []
+    for j in range(1, chips):
+        send_upd.append(remote(upd.at[rep], upd.at[rep], upd_sem, (j - 1,), peer(j)))
+        send_upd[j - 1].start()
+    forward = [remote(upd.at[rep], upd.at[rep], fwd_sem, (0,), sibling)]
+    forward[0].start()
+    load_loc.wait()
+    load_glob.wait()
+
+    def merge(index):
+        cols = columns(index)
+        later = glob_s[:, cols] - upd[index].astype(jnp.float32)
+        merged = merge_weight * loc_s[:, cols].astype(jnp.float32) + (1.0 - merge_weight) * later
+        loc_out[:, cols] = merged.astype(jnp.bfloat16)
+
+    merge(rep)
+    for j in range(1, chips):
+        send_upd[j - 1].wait_recv()
+        came = ((chip - j + chips) % chips) * 2 + core
+        forward.append(remote(upd.at[came], upd.at[came], fwd_sem, (j,), sibling))
+        forward[j].start()
+        merge(came)
+    for j in range(chips):
+        forward[j].wait_recv()
+        merge(((chip - j + chips) % chips) * 2 + 1 - core)
+    store_loc = pltpu.make_async_copy(loc_out, local_next.at[0], out_sem.at[1])
+    store_loc.start()
+
+    stores = []
+    for c in range(chunks):
+        part = pl.ds(c * chunk_rows, chunk_rows)
+        for t in range(tiles):
+            send_back[c * tiles + t].wait_recv()
+            cols = pl.ds(t * tile_cols, tile_cols)
+            out_s[part, cols] = (sum_own[part, cols] + back[c, t].astype(jnp.float32)).astype(
+                jnp.bfloat16
+            )
+        stores.append(pltpu.make_async_copy(out_s.at[part], moe_out.at[part], out_sem.at[2 + c]))
+        stores[c].start()
+
+    for copy in [send_mix, to_sib, to_other] + send_tok + send_sib + send_far + send_sq + send_back:
+        copy.wait_send()
+    for copy in send_upd + forward:
+        copy.wait_send()
+    for copy in stores + [store_mom, store_loc]:
+        copy.wait()
+
+
+def fused(
+    reps,
+    tokens,
+    routes,
+    route_weight,
+    w_gate,
+    w_up,
+    w_down,
+    pseudo_grad,
+    global_params,
+    momentum,
+    local_params,
+):
+    rows, width = tokens.shape
+    experts, _, hidden = w_gate.shape
+    frag_rows = momentum.shape[0]
+    chips = reps // 2
+    chunks, tiles = 2, 4
+    f32, bf16 = jnp.float32, jnp.bfloat16
+    anywhere = pl.BlockSpec(memory_space=pl.ANY)
+    in_vmem = pl.BlockSpec(memory_space=pltpu.VMEM)
+    dma = pltpu.SemaphoreType.DMA
+    block = (frag_rows, LANES)
+    returned = (chunks, tiles, rows // chunks, width // tiles)
+    return pl.pallas_call(
+        functools.partial(kernel, reps),
+        out_shape=(
+            jax.ShapeDtypeStruct(tokens.shape, tokens.dtype),
+            jax.ShapeDtypeStruct(momentum.shape, momentum.dtype),
+            jax.ShapeDtypeStruct(local_params.shape, local_params.dtype),
+        ),
+        in_specs=[anywhere, in_vmem, in_vmem] + [anywhere] * 7,
+        out_specs=(anywhere,) * 3,
+        scratch_shapes=[
+            pltpu.VMEM(w_gate.shape, bf16),
+            pltpu.VMEM(w_up.shape, bf16),
+            pltpu.VMEM((experts * hidden, width), bf16),
+            pltpu.VMEM(tokens.shape, bf16),
+            pltpu.VMEM(tokens.shape, bf16),
+            pltpu.VMEM((rows, LANES), f32),
+            pltpu.VMEM((8, rows), f32),
+            pltpu.VMEM((8, rows), f32),
+            pltpu.VMEM((rows, LANES), f32),
+            pltpu.VMEM((rows, LANES), f32),
+            pltpu.VMEM((rows, experts * hidden), bf16),
+            pltpu.VMEM((rows, experts * hidden), bf16),
+            pltpu.VMEM((rows, width), f32),
+            pltpu.VMEM(returned, bf16),
+            pltpu.VMEM(returned, bf16),
+            pltpu.VMEM(tokens.shape, bf16),
+            pltpu.VMEM((chips,) + block, f32),
+            pltpu.VMEM((chips,) + block, f32),
+            pltpu.VMEM((chips,) + block, f32),
+            pltpu.VMEM((chips - 1,) + block, f32),
+            pltpu.VMEM((8, LANES), f32),
+            pltpu.VMEM((chips - 1, 8, LANES), f32),
+            pltpu.VMEM((8, LANES), f32),
+            pltpu.VMEM((8, LANES), f32),
+            pltpu.VMEM((8, LANES), f32),
+            pltpu.VMEM((8, LANES), f32),
+            pltpu.VMEM(block, f32),
+            pltpu.VMEM((frag_rows, width), f32),
+            pltpu.VMEM((frag_rows, width), bf16),
+            pltpu.VMEM((reps,) + block, bf16),
+            pltpu.VMEM(block, f32),
+            pltpu.VMEM((frag_rows, width), bf16),
+            dma((3, experts)),
+            dma((4,)),
+            dma((2 + chunks,)),
+            dma((chips,)),
+            dma((2, chunks)),
+            dma((2, 1)),
+            dma((2, chunks, tiles)),
+            dma((2, chips)),
+            dma((2, chips - 1)),
+            dma((2, chips - 1)),
+            dma((2, 2)),
+            dma((2, chips - 1)),
+            dma((2, chips)),
+        ],
+        compiler_params=pltpu.CompilerParams(
+            collective_id=0, has_side_effects=True, vmem_limit_bytes=56 * 1024 * 1024
+        ),
+        cost_estimate=pl.CostEstimate(
+            flops=12 * rows * experts * hidden * width,
+            bytes_accessed=6 * experts * hidden * width,
+            transcendentals=0,
+        ),
+    )(
+        tokens,
+        routes.T,
+        route_weight.T,
+        w_gate,
+        w_up,
+        w_down,
+        pseudo_grad,
+        global_params,
+        momentum,
+        local_params,
+    )
+
+
 def solution(mesh):
     in_specs = (
         P(("rep", "shard"), None),
@@ -92,4 +527,14 @@
         P("rep", "shard", None),
     )
     out_specs = (P(("rep", "shard"), None), P("shard", "rep"), P("rep", "shard", None))
-    return jax.shard_map(local, mesh=mesh, in_specs=in_specs, out_specs=out_specs, check_vma=False)
+    reps, shards = mesh.shape["rep"], mesh.shape["shard"]
+
+    def step(*arrays):
+        tokens, w_gate, momentum = arrays[0], arrays[3], arrays[8]
+        pairs = shards == 2 and reps % 2 == 0 and reps >= 4
+        aligned = momentum.shape[1] == LANES and tokens.shape[0] == LANES
+        if pairs and aligned and w_gate.shape[0] * shards == 8:
+            return fused(reps, *arrays)
+        return local(*arrays)
+
+    return jax.shard_map(step, mesh=mesh, in_specs=in_specs, out_specs=out_specs, check_vma=False)

time: 184 us -> 51 us (0.28)
  waiting for transfers between devices: 86.9 us -> 0 us
  Pallas kernels: 0 us -> 44.3 us
  blocking collectives: 32.3 us -> 0 us
  matrix products: 21.8 us -> 0 us
  between operations: 14.9 us -> 0.64 us
  other arithmetic: 9.08 us -> 0 us
  starting transfers between devices: 8.32 us -> 0 us
  local copies, waits for them, and re-layouts: 9.91 us -> 5.07 us
    psum x1 -> x0, waiting for transfers between devices: 72 us -> none  [local(): delta_total = lax.psum(own_delta, 'rep')]
    pallas_call x0 -> x1, Pallas kernels: none -> 44.3 us  [fused(): pl.pallas_call(functools.partial(kernel, reps), out_shape=(jax.ShapeDtype...]
    all_gather x1 -> x0, blocking collectives: 26.8 us -> none  [local(): full_momentum = lax.all_gather(momentum, 'rep', axis=1, tiled=True)]
    dot_general x3 -> x0, matrix products: 21.8 us -> none  [the longest x1 13.5 us: local(): jnp.einsum('spcf,pfd->spcd', hidden, w_down, preferred_element_type=jnp.f...]
    all_to_all x2 -> x0, waiting for transfers between devices: 14.2 us -> none  [the longest x1 14.2 us: local(): lax.all_to_all(result, 'shard', split_axis=0, concat_axis=0, tiled=True)]
    all_to_all x2 -> x0, starting transfers between devices: 8.32 us -> none  [the longest x1 4.34 us: local(): lax.all_to_all(outgoing, 'shard', split_axis=0, concat_axis=0, tiled=True)]
    reduce_sum x4 -> x0, other arithmetic: 6.03 us -> none  [the longest x1 3.93 us: local(): jnp.sum(route_weight[:, :, None] * picked, axis=1).astype(jnp.bfloat16)]
    psum x1 -> x0, blocking collectives: 5.55 us -> none  [local(): square_sum = lax.psum(jnp.sum(mean_delta * mean_delta), 'shard')]
  transfers between devices with their start and end apart: 3 -> 0, of which waited for: 2 -> 0; matrix products, arithmetic and copies ran while one was open for 3% -> 0% of each run, Pallas kernels for 0% -> 0%
where the time goes in v1:
time: 51 us; the launch traced here: 50 us
  Pallas kernels  44.3 us (87%)
  local copies, waits for them, and re-layouts  5.07 us (10%)
  between operations  0.64 us (1%)
    pallas_call x1, Pallas kernels, fused(): pl.pallas_call(functools.partial(kernel, reps), out_shape=(jax.ShapeDtype...  44.3 us
    unnamed x3, local copies, waits for them, and re-layouts  5.07 us

profile of v1, /device:TPU:0, one launch (start us, length us, event | category | flops | bytes accessed | tf_op | source)
XLA Modules:
  0.0 50.0 jit_solution(9658106787262488624)
XLA Ops:
  0.6 44.3 %shard_map.121 = (bf16[128,2048]{1,0:T(8,128)(2,1)}, f32[96,128]{1,0:T(8,128)}, bf16[1,96,2048]{2,1,0:T(8,128)(2,1)}) custom-call(bf16[128,2048]{1,0:T(8,128)(2,1)} %tokens.1, s32[2,128]{1,0:T(2,128)} %bitcast.2, f32[2,128]{1,0:T(2,128)} %bitcast.3, bf16[4,2048,768]{2,1,0:T(8,128)(2,1)} %w_gate.1, bf16[4,2048,768]{2,1,0:T(8,128)(2,1)} %w_up.1, ...), custom_call_target="tpu_custom_call" | custom-call | flops 9663676416 | bytes 37748736 | tf_op jit(solution)/shard_map/pallas_call | solution.py:438
  44.9 1.9 %copy.16 = bf16[128,2048]{1,0:T(8,128)(2,1)} copy(bf16[128,2048]{1,0:T(8,128)(2,1)} %get-tuple-element.6) | data formatting | bytes 1048576
  46.8 1.4 %copy.17 = f32[96,128]{1,0:T(8,128)} copy(f32[96,128]{1,0:T(8,128)} %get-tuple-element.7) | data formatting | bytes 98304
  48.3 1.8 %copy.18 = bf16[1,96,2048]{2,1,0:T(8,128)(2,1)} copy(bf16[1,96,2048]{2,1,0:T(8,128)(2,1)} %get-tuple-element.8) | data formatting | bytes 786432

commit v2 on v1

--- a/solution.py
+++ b/solution.py
@@ -109,6 +109,7 @@
     mix_own,
     mix_send,
     mix_far,
+    mix_got,
     col_own,
     col_far,
     hid_own,
@@ -127,6 +128,7 @@
     sq_sib,
     sq_half,
     sq_other,
+    mean_s,
     mom_s,
     glob_s,
     loc_s,
@@ -144,6 +146,7 @@
     far_sem,
     sq_sem,
     one_sem,
+    mom_sem,
     upd_sem,
     fwd_sem,
 ):
@@ -186,6 +189,7 @@
         for k in range(chips)
     ]
 
+    load_mom.start()
     load_tok.start()
     for copy in weights[:2]:
         copy.start()
@@ -230,11 +234,16 @@
             )
         )
         send_sib[k].start()
+    load_mom.wait()
+    upd[rep, 0] = mom_s[...].astype(jnp.bfloat16)
+    send_mom = []
+    for j in range(1, chips):
+        send_mom.append(remote(upd.at[rep, 0], upd.at[rep, 0], mom_sem, (j - 1,), peer(j)))
+        send_mom[j - 1].start()
     for copy in weights[2:]:
         copy.start()
     load_loc.start()
     load_glob.start()
-    load_mom.start()
 
     def gate_up(tok, part, col, hid, e):
         tok_part = tok[part, :]
@@ -252,15 +261,18 @@
 
     whole = pl.ds(0, rows)
 
+    def own_rows(e):
+        pick(mix_own, col_own, e)
+        gate_up(own_tok, whole, col_own, hid_own, e)
+
     def own_step(e, carry):
         pltpu.make_async_copy(w_gate.at[e], gate_s.at[e], w_sem.at[0, e]).wait()
         pltpu.make_async_copy(w_up.at[e], up_s.at[e], w_sem.at[1, e]).wait()
-        pick(mix_own, col_own, e)
-        gate_up(own_tok, whole, col_own, hid_own, e)
+        own_rows(e)
         return carry
 
     load_tok.wait()
-    lax.fori_loop(0, experts // 2, own_step, 0)
+    lax.fori_loop(0, 1, own_step, 0)
 
     for copy in load_grad:
         copy.wait()
@@ -279,17 +291,17 @@
         )
         send_far[j - 1].start()
 
-    lax.fori_loop(experts // 2, experts, own_step, 0)
+    lax.fori_loop(1, experts - 1, own_step, 0)
 
     send_mix.wait_recv()
-    mix_own[...] = jnp.concatenate([mix_far[...], rest], axis=0).T
+    mix_got[...] = jnp.concatenate([mix_far[...], rest], axis=0).T
 
     def far_rows(c):
         part = pl.ds(c * chunk_rows, chunk_rows)
         send_tok[c].wait_recv()
 
         def far_step(e, carry):
-            pick(mix_own, col_far, e)
+            pick(mix_got, col_far, e)
             gate_up(far_tok, part, col_far, hid_far, e)
             return carry
 
@@ -312,13 +324,16 @@
             copy.start()
             send_back.append(copy)
 
+    for copy in weights[2 * experts - 2 : 2 * experts]:
+        copy.wait()
     far_rows(0)
     for copy in weights[2 * experts :]:
         copy.wait()
     far_down(0)
-    for c in range(1, chunks):
+    for c in range(1, chunks - 1):
         far_rows(c)
         far_down(c)
+    far_rows(chunks - 1)
 
     for copy in send_far:
         copy.wait_recv()
@@ -331,14 +346,21 @@
     for i in range(8, frag_rows, 8):
         square = square + squares[i : i + 8]
     sq_own[...] = square
+    mean_s[...] = mean
+    upd[rep, 1] = mean.astype(jnp.bfloat16)
+    send_upd = []
+    for j in range(1, chips):
+        send_upd.append(remote(upd.at[rep, 1], upd.at[rep, 1], upd_sem, (j - 1,), peer(j)))
+        send_upd[j - 1].start()
+    forward = [remote(upd.at[rep], upd.at[rep], fwd_sem, (0,), sibling)]
+    forward[0].start()
     send_sq = []
     for j in range(1, chips):
         send_sq.append(remote(sq_own, sq_far.at[j - 1], sq_sem, (j - 1,), peer(j)))
         send_sq[j - 1].start()
-
-    for t in range(tiles):
-        sum_own[:, t * tile_cols : (t + 1) * tile_cols] = down(hid_own[...], t)
-
+    far_down(chunks - 1)
+
+    own_rows(experts - 1)
     for copy in send_sq:
         copy.wait_recv()
     square = sq_own[...]
@@ -347,52 +369,28 @@
     sq_chip[...] = square
     to_sib = remote(sq_chip, sq_sib, one_sem, (0,), sibling)
     to_sib.start()
+
+    def own_down(t):
+        sum_own[:, t * tile_cols : (t + 1) * tile_cols] = down(hid_own[...], t)
+
+    own_down(0)
     to_sib.wait_recv()
     sq_half[...] = sq_chip[...] + sq_sib[...]
     to_other = remote(sq_half, sq_other, one_sem, (1,), partner)
     to_other.start()
-    to_other.wait_recv()
-    entries = float(frag_rows * 2 * width)
-    square_sum = jnp.sum(sq_half[...] + sq_other[...])
-    clip_factor = jnp.minimum(1.0, lax.rsqrt(square_sum / entries + clip_epsilon))
-    clipped = clip_factor * mean
-    load_mom.wait()
-    fresh = outer_momentum * mom_s[...] + clipped
-    mom_out[...] = fresh
-    store_mom = pltpu.make_async_copy(mom_out, momentum_next, out_sem.at[0])
-    store_mom.start()
-    upd[rep] = (outer_rate * (outer_momentum * fresh + clipped)).astype(jnp.bfloat16)
-
-    send_upd = []
-    for j in range(1, chips):
-        send_upd.append(remote(upd.at[rep], upd.at[rep], upd_sem, (j - 1,), peer(j)))
-        send_upd[j - 1].start()
-    forward = [remote(upd.at[rep], upd.at[rep], fwd_sem, (0,), sibling)]
-    forward[0].start()
-    load_loc.wait()
-    load_glob.wait()
-
-    def merge(index):
-        cols = columns(index)
-        later = glob_s[:, cols] - upd[index].astype(jnp.float32)
-        merged = merge_weight * loc_s[:, cols].astype(jnp.float32) + (1.0 - merge_weight) * later
-        loc_out[:, cols] = merged.astype(jnp.bfloat16)
-
-    merge(rep)
-    for j in range(1, chips):
+    for t in range(1, tiles):
+        own_down(t)
+
+    for j in range(1, chips):
+        send_mom[j - 1].wait_recv()
         send_upd[j - 1].wait_recv()
         came = ((chip - j + chips) % chips) * 2 + core
         forward.append(remote(upd.at[came], upd.at[came], fwd_sem, (j,), sibling))
         forward[j].start()
-        merge(came)
-    for j in range(chips):
-        forward[j].wait_recv()
-        merge(((chip - j + chips) % chips) * 2 + 1 - core)
-    store_loc = pltpu.make_async_copy(loc_out, local_next.at[0], out_sem.at[1])
-    store_loc.start()
 
     stores = []
-    for c in range(chunks):
+
+    def combine(c):
         part = pl.ds(c * chunk_rows, chunk_rows)
         for t in range(tiles):
             send_back[c * tiles + t].wait_recv()
@@ -403,11 +401,57 @@
         stores.append(pltpu.make_async_copy(out_s.at[part], moe_out.at[part], out_sem.at[2 + c]))
         stores[c].start()
 
+    for c in range(chunks - 1):
+        combine(c)
+
+    to_other.wait_recv()
+    entries = float(frag_rows * 2 * width)
+    square_sum = jnp.sum(sq_half[...] + sq_other[...])
+    clip_factor = jnp.minimum(1.0, lax.rsqrt(square_sum / entries + clip_epsilon))
+    mom_out[...] = outer_momentum * mom_s[...] + clip_factor * mean_s[...]
+    store_mom = pltpu.make_async_copy(mom_out, momentum_next, out_sem.at[0])
+    store_mom.start()
+    load_loc.wait()
+    load_glob.wait()
+
+    def merge(index):
+        cols = columns(index)
+        clipped = clip_factor * upd[index, 1].astype(jnp.float32)
+        fresh = outer_momentum * upd[index, 0].astype(jnp.float32) + clipped
+        later = glob_s[:, cols] - outer_rate * (outer_momentum * fresh + clipped)
+        merged = merge_weight * loc_s[:, cols].astype(jnp.float32) + (1.0 - merge_weight) * later
+        loc_out[:, cols] = merged.astype(jnp.bfloat16)
+
+    for j in range(chips):
+        merge(((chip - j + chips) % chips) * 2 + core)
+    for j in range(chips):
+        forward[j].wait_recv()
+        merge(((chip - j + chips) % chips) * 2 + 1 - core)
+    store_loc = pltpu.make_async_copy(loc_out, local_next.at[0], out_sem.at[1])
+    store_loc.start()
+
+    combine(chunks - 1)
+
     for copy in [send_mix, to_sib, to_other] + send_tok + send_sib + send_far + send_sq + send_back:
         copy.wait_send()
-    for copy in send_upd + forward:
+    for copy in send_mom + send_upd + forward:
         copy.wait_send()
     for copy in stores + [store_mom, store_loc]:
+        copy.wait()
+
+
+def closing(moe_in, momentum_in, local_in, moe_out, momentum_next, local_next, sems):
+    copies = []
+    for source, target in ((moe_in, moe_out), (local_in.at[0], local_next.at[0])):
+        half = source.shape[0] // 2
+        for k in range(2):
+            part = pl.ds(k * half, half)
+            sem = sems.at[len(copies)]
+            copies.append(pltpu.make_async_copy(source.at[part], target.at[part], sem))
+    copies.append(pltpu.make_async_copy(momentum_in, momentum_next, sems.at[4]))
+    for copy in copies:
+        copy.start()
+    for copy in copies:
         copy.wait()
 
 
@@ -435,13 +479,14 @@
     dma = pltpu.SemaphoreType.DMA
     block = (frag_rows, LANES)
     returned = (chunks, tiles, rows // chunks, width // tiles)
-    return pl.pallas_call(
+    out_shape = (
+        jax.ShapeDtypeStruct(tokens.shape, tokens.dtype),
+        jax.ShapeDtypeStruct(momentum.shape, momentum.dtype),
+        jax.ShapeDtypeStruct(local_params.shape, local_params.dtype),
+    )
+    results = pl.pallas_call(
         functools.partial(kernel, reps),
-        out_shape=(
-            jax.ShapeDtypeStruct(tokens.shape, tokens.dtype),
-            jax.ShapeDtypeStruct(momentum.shape, momentum.dtype),
-            jax.ShapeDtypeStruct(local_params.shape, local_params.dtype),
-        ),
+        out_shape=out_shape,
         in_specs=[anywhere, in_vmem, in_vmem] + [anywhere] * 7,
         out_specs=(anywhere,) * 3,
         scratch_shapes=[
@@ -453,6 +498,7 @@
             pltpu.VMEM((rows, LANES), f32),
             pltpu.VMEM((8, rows), f32),
             pltpu.VMEM((8, rows), f32),
+            pltpu.VMEM((rows, LANES), f32),
             pltpu.VMEM((rows, LANES), f32),
             pltpu.VMEM((rows, LANES), f32),
             pltpu.VMEM((rows, experts * hidden), bf16),
@@ -472,9 +518,10 @@
             pltpu.VMEM((8, LANES), f32),
             pltpu.VMEM((8, LANES), f32),
             pltpu.VMEM(block, f32),
+            pltpu.VMEM(block, f32),
             pltpu.VMEM((frag_rows, width), f32),
             pltpu.VMEM((frag_rows, width), bf16),
-            pltpu.VMEM((reps,) + block, bf16),
+            pltpu.VMEM((reps, 2) + block, bf16),
             pltpu.VMEM(block, f32),
             pltpu.VMEM((frag_rows, width), bf16),
             dma((3, experts)),
@@ -488,6 +535,7 @@
             dma((2, chips - 1)),
             dma((2, chips - 1)),
             dma((2, 2)),
+            dma((2, chips - 1)),
             dma((2, chips - 1)),
             dma((2, chips)),
         ],
@@ -511,6 +559,14 @@
         momentum,
         local_params,
     )
+    return pl.pallas_call(
+        closing,
+        out_shape=out_shape,
+        in_specs=[anywhere] * 3,
+        out_specs=(anywhere,) * 3,
+        scratch_shapes=[dma((5,))],
+        compiler_params=pltpu.CompilerParams(vmem_limit_bytes=60 * 1024 * 1024),
+    )(*results)
 
 
 def solution(mesh):

time: 51 us -> 70.2 us (1.38); the launches traced: 50 us -> 70.1 us
  Pallas kernels: 44.3 us -> 69.4 us
  local copies, waits for them, and re-layouts: 5.07 us -> 0 us
    pallas_call x1 -> x2, Pallas kernels: 44.3 us -> 69.4 us  [the longest x1 39 us: fused(): pl.pallas_call(functools.partial(kernel, reps), out_shape=out_shape, in_s...]
    unnamed x3 -> x0, local copies, waits for them, and re-layouts: 5.07 us -> none
where the time goes in v2:
time: 70.2 us; the launch traced here: 70.1 us
  Pallas kernels  69.4 us (99%)
    pallas_call x1, Pallas kernels, fused(): pl.pallas_call(functools.partial(kernel, reps), out_shape=out_shape, in_s...  39 us
    pallas_call x1, Pallas kernels, fused(): pl.pallas_call(closing, out_shape=out_shape, in_specs=[anywhere] * 3, out...  30.4 us

profile of v2, /device:TPU:0, one launch (start us, length us, event | category | flops | bytes accessed | tf_op | source)
XLA Modules:
  0.0 70.1 jit_solution(352487926257985525)
XLA Ops:
  0.6 39.0 %shard_map.121 = (bf16[128,2048]{1,0:T(8,128)(2,1)}, f32[96,128]{1,0:T(8,128)}, bf16[1,96,2048]{2,1,0:T(8,128)(2,1)}) custom-call(bf16[128,2048]{1,0:T(8,128)(2,1)} %tokens.1, s32[2,128]{1,0:T(2,128)} %bitcast.2, f32[2,128]{1,0:T(2,128)} %bitcast.3, bf16[4,2048,768]{2,1,0:T(8,128)(2,1)} %w_gate.1, bf16[4,2048,768]{2,1,0:T(8,128)(2,1)} %w_up.1, ...), custom_call_target="tpu_custom_call" | custom-call | flops 9663676416 | bytes 37748736 | tf_op jit(solution)/shard_map/pallas_call | solution.py:487
  39.6 30.4 %shard_map.122 = (bf16[128,2048]{1,0:T(8,128)(2,1)}, f32[96,128]{1,0:T(8,128)}, bf16[1,96,2048]{2,1,0:T(8,128)(2,1)}) custom-call(bf16[128,2048]{1,0:T(8,128)(2,1)} %get-tuple-element.6.moe_in, f32[96,128]{1,0:T(8,128)} %get-tuple-element.7.momentum_in, bf16[1,96,2048]{2,1,0:T(8,128)(2,1)} %get-tuple-element.8.local_in), custom_call_target="tpu_custom_call" | custom-call | tf_op jit(solution)/shard_map/pallas_call | solution.py:562

commit v3 on v2

--- a/solution.py
+++ b/solution.py
@@ -104,16 +104,11 @@
     gate_s,
     up_s,
     down_s,
-    own_tok,
-    far_tok,
-    mix_own,
+    tok,
+    mix_all,
     mix_send,
     mix_far,
-    mix_got,
-    col_own,
-    col_far,
-    hid_own,
-    hid_far,
+    hid,
     sum_own,
     back_send,
     back,
@@ -178,7 +173,7 @@
         weights.append(
             pltpu.make_async_copy(w_down.at[e], down_s.at[pl.ds(e * hidden, hidden)], w_sem.at[2, e])
         )
-    load_tok = pltpu.make_async_copy(tokens, own_tok, in_sem.at[0])
+    load_tok = pltpu.make_async_copy(tokens, tok.at[pl.ds(0, rows)], in_sem.at[0])
     load_glob = pltpu.make_async_copy(global_params, glob_s, in_sem.at[1])
     load_mom = pltpu.make_async_copy(momentum, mom_s, in_sem.at[2])
     load_loc = pltpu.make_async_copy(local_params.at[0], loc_s, in_sem.at[3])
@@ -202,7 +197,7 @@
         mix = mix + jnp.where(ids == routes[k : k + 1, :], route_weight[k : k + 1, :], 0.0)
     mix_send[...] = mix
     rest = jnp.zeros((LANES - 8, rows), jnp.float32)
-    mix_own[...] = jnp.concatenate([mix, rest], axis=0).T
+    mix_all[pl.ds(0, rows), :] = jnp.concatenate([mix, rest], axis=0).T
 
     barrier = pltpu.get_barrier_semaphore()
     for device in [partner, sibling] + [peer(j) for j in range(1, chips)]:
@@ -224,7 +219,8 @@
     send_tok = []
     for c in range(chunks):
         part = pl.ds(c * chunk_rows, chunk_rows)
-        send_tok.append(remote(tokens.at[part], far_tok.at[part], tok_sem, (c,), partner))
+        there = tok.at[pl.ds(rows + c * chunk_rows, chunk_rows)]
+        send_tok.append(remote(tokens.at[part], there, tok_sem, (c,), partner))
         send_tok[c].start()
     send_sib = []
     for k in range(chips):
@@ -245,34 +241,34 @@
     load_loc.start()
     load_glob.start()
 
-    def gate_up(tok, part, col, hid, e):
+    def gate_up(start, count, e):
+        part = pl.ds(start, count)
+        lanes = lax.broadcasted_iota(jnp.int32, (count, LANES), 1)
+        chosen = jnp.where(lanes == shard * experts + e, mix_all[part, :], 0.0)
+        scale = jnp.sum(chosen, axis=1, keepdims=True)
         tok_part = tok[part, :]
-        scale = col[part, pl.ds(0, 1)]
         for f in range(0, hidden, 256):
             gate = jnp.dot(tok_part, gate_s[e, :, f : f + 256], preferred_element_type=jnp.float32)
             upward = jnp.dot(tok_part, up_s[e, :, f : f + 256], preferred_element_type=jnp.float32)
             value = gate / (1.0 + jnp.exp(-gate)) * upward * scale
             hid[part, pl.ds(pl.multiple_of(e * hidden + f, LANES), 256)] = value.astype(jnp.bfloat16)
 
-    def pick(mix_ref, col, e):
-        lanes = lax.broadcasted_iota(jnp.int32, (rows, LANES), 1)
-        chosen = jnp.where(lanes == shard * experts + e, mix_ref[...], 0.0)
-        col[...] = jnp.broadcast_to(jnp.sum(chosen, axis=1, keepdims=True), (rows, LANES))
-
-    whole = pl.ds(0, rows)
-
-    def own_rows(e):
-        pick(mix_own, col_own, e)
-        gate_up(own_tok, whole, col_own, hid_own, e)
-
-    def own_step(e, carry):
+    def weights_in(e):
         pltpu.make_async_copy(w_gate.at[e], gate_s.at[e], w_sem.at[0, e]).wait()
         pltpu.make_async_copy(w_up.at[e], up_s.at[e], w_sem.at[1, e]).wait()
-        own_rows(e)
-        return carry
-
+
+    def steps(start, count, first, last, fresh):
+        def one(e, carry):
+            if fresh:
+                weights_in(e)
+            gate_up(start, count, e)
+            return carry
+
+        lax.fori_loop(first, last, one, 0)
+
+    early = experts // 2
     load_tok.wait()
-    lax.fori_loop(0, 1, own_step, 0)
+    steps(0, rows, 0, 1, True)
 
     for copy in load_grad:
         copy.wait()
@@ -291,49 +287,35 @@
         )
         send_far[j - 1].start()
 
-    lax.fori_loop(1, experts - 1, own_step, 0)
+    steps(0, rows, 1, early, True)
 
     send_mix.wait_recv()
-    mix_got[...] = jnp.concatenate([mix_far[...], rest], axis=0).T
-
-    def far_rows(c):
-        part = pl.ds(c * chunk_rows, chunk_rows)
-        send_tok[c].wait_recv()
-
-        def far_step(e, carry):
-            pick(mix_got, col_far, e)
-            gate_up(far_tok, part, col_far, hid_far, e)
-            return carry
-
-        lax.fori_loop(0, experts, far_step, 0)
-
-    def down(hid_part, t):
+    mix_all[pl.ds(rows, rows), :] = jnp.concatenate([mix_far[...], rest], axis=0).T
+    send_tok[0].wait_recv()
+    steps(rows, chunk_rows, 0, early, False)
+    steps(0, rows + chunk_rows, early, experts, True)
+    for copy in weights[2 * experts :]:
+        copy.wait()
+
+    def down(start, count, t):
         return jnp.dot(
-            hid_part,
+            hid[pl.ds(start, count), :],
             down_s[:, t * tile_cols : (t + 1) * tile_cols],
             preferred_element_type=jnp.float32,
         )
 
     send_back = []
 
-    def far_down(c):
-        part = pl.ds(c * chunk_rows, chunk_rows)
-        for t in range(tiles):
-            back_send[c, t] = down(hid_far[part, :], t).astype(jnp.bfloat16)
-            copy = remote(back_send.at[c, t], back.at[c, t], back_sem, (c, t), partner)
-            copy.start()
-            send_back.append(copy)
-
-    for copy in weights[2 * experts - 2 : 2 * experts]:
-        copy.wait()
-    far_rows(0)
-    for copy in weights[2 * experts :]:
-        copy.wait()
-    far_down(0)
-    for c in range(1, chunks - 1):
-        far_rows(c)
-        far_down(c)
-    far_rows(chunks - 1)
+    def give_back(c, t, value):
+        back_send[c, t] = value.astype(jnp.bfloat16)
+        copy = remote(back_send.at[c, t], back.at[c, t], back_sem, (c, t), partner)
+        copy.start()
+        send_back.append(copy)
+
+    for t in range(tiles):
+        both = down(0, rows + chunk_rows, t)
+        give_back(0, t, both[rows:])
+        sum_own[:, t * tile_cols : (t + 1) * tile_cols] = both[:rows]
 
     for copy in send_far:
         copy.wait_recv()
@@ -358,9 +340,8 @@
     for j in range(1, chips):
         send_sq.append(remote(sq_own, sq_far.at[j - 1], sq_sem, (j - 1,), peer(j)))
         send_sq[j - 1].start()
-    far_down(chunks - 1)
-
-    own_rows(experts - 1)
+    send_tok[1].wait_recv()
+    steps(rows + chunk_rows, chunk_rows, 0, early, False)
     for copy in send_sq:
         copy.wait_recv()
     square = sq_own[...]
@@ -369,17 +350,13 @@
     sq_chip[...] = square
     to_sib = remote(sq_chip, sq_sib, one_sem, (0,), sibling)
     to_sib.start()
-
-    def own_down(t):
-        sum_own[:, t * tile_cols : (t + 1) * tile_cols] = down(hid_own[...], t)
-
-    own_down(0)
+    steps(rows + chunk_rows, chunk_rows, early, experts, False)
     to_sib.wait_recv()
     sq_half[...] = sq_chip[...] + sq_sib[...]
     to_other = remote(sq_half, sq_other, one_sem, (1,), partner)
     to_other.start()
-    for t in range(1, tiles):
-        own_down(t)
+    for t in range(tiles):
+        give_back(1, t, down(rows + chunk_rows, chunk_rows, t))
 
     for j in range(1, chips):
         send_mom[j - 1].wait_recv()
@@ -440,19 +417,23 @@
         copy.wait()
 
 
-def closing(moe_in, momentum_in, local_in, moe_out, momentum_next, local_next, sems):
-    copies = []
-    for source, target in ((moe_in, moe_out), (local_in.at[0], local_next.at[0])):
+def closing(moe_in, momentum_in, local_in, moe_out, momentum_next, local_next, moe_s, mom_s, loc_s, sems):
+    pieces = [(momentum_in, mom_s, momentum_next)]
+    for source, middle, target in ((moe_in, moe_s, moe_out), (local_in.at[0], loc_s, local_next.at[0])):
         half = source.shape[0] // 2
         for k in range(2):
             part = pl.ds(k * half, half)
-            sem = sems.at[len(copies)]
-            copies.append(pltpu.make_async_copy(source.at[part], target.at[part], sem))
-    copies.append(pltpu.make_async_copy(momentum_in, momentum_next, sems.at[4]))
-    for copy in copies:
-        copy.start()
-    for copy in copies:
-        copy.wait()
+            pieces.append((source.at[part], middle.at[part], target.at[part]))
+    loads, stores = [], []
+    for k, (source, middle, target) in enumerate(pieces):
+        loads.append(pltpu.make_async_copy(source, middle, sems.at[0, k]))
+        stores.append(pltpu.make_async_copy(middle, target, sems.at[1, k]))
+        loads[k].start()
+    for load, store in zip(loads, stores):
+        load.wait()
+        store.start()
+    for store in stores:
+        store.wait()
 
 
 def fused(
@@ -493,16 +474,11 @@
             pltpu.VMEM(w_gate.shape, bf16),
             pltpu.VMEM(w_up.shape, bf16),
             pltpu.VMEM((experts * hidden, width), bf16),
-            pltpu.VMEM(tokens.shape, bf16),
-            pltpu.VMEM(tokens.shape, bf16),
-            pltpu.VMEM((rows, LANES), f32),
+            pltpu.VMEM((2 * rows, width), bf16),
+            pltpu.VMEM((2 * rows, LANES), f32),
             pltpu.VMEM((8, rows), f32),
             pltpu.VMEM((8, rows), f32),
-            pltpu.VMEM((rows, LANES), f32),
-            pltpu.VMEM((rows, LANES), f32),
-            pltpu.VMEM((rows, LANES), f32),
-            pltpu.VMEM((rows, experts * hidden), bf16),
-            pltpu.VMEM((rows, experts * hidden), bf16),
+            pltpu.VMEM((2 * rows, experts * hidden), bf16),
             pltpu.VMEM((rows, width), f32),
             pltpu.VMEM(returned, bf16),
             pltpu.VMEM(returned, bf16),
@@ -564,7 +540,12 @@
         out_shape=out_shape,
         in_specs=[anywhere] * 3,
         out_specs=(anywhere,) * 3,
-        scratch_shapes=[dma((5,))],
+        scratch_shapes=[
+            pltpu.VMEM(tokens.shape, bf16),
+            pltpu.VMEM(block, f32),
+            pltpu.VMEM((frag_rows, width), bf16),
+            dma((2, 5)),
+        ],
         compiler_params=pltpu.CompilerParams(vmem_limit_bytes=60 * 1024 * 1024),
     )(*results)
 

time: 70.2 us -> 42.6 us (0.61)
  Pallas kernels: 69.4 us -> 41.8 us
    pallas_call x1, Pallas kernels: 30.4 us -> 1.98 us  [fused(): pl.pallas_call(closing, out_shape=out_shape, in_specs=[anywhere] * 3, out...]
    pallas_call x1, Pallas kernels: 39 us -> 39.8 us  [fused(): pl.pallas_call(functools.partial(kernel, reps), out_shape=out_shape, in_s...]
where the time goes in v3:
time: 42.6 us; the launch traced here: 42.4 us
  Pallas kernels  41.8 us (98%)
  between operations  0.64 us (2%)
    pallas_call x1, Pallas kernels, fused(): pl.pallas_call(functools.partial(kernel, reps), out_shape=out_shape, in_s...  39.8 us
    pallas_call x1, Pallas kernels, fused(): pl.pallas_call(closing, out_shape=out_shape, in_specs=[anywhere] * 3, out...  1.98 us

profile of v3, /device:TPU:0, one launch (start us, length us, event | category | flops | bytes accessed | tf_op | source)
XLA Modules:
  0.0 42.4 jit_solution(17033085647855821872)
XLA Ops:
  0.6 39.8 %shard_map.121 = (bf16[128,2048]{1,0:T(8,128)(2,1)}, f32[96,128]{1,0:T(8,128)}, bf16[1,96,2048]{2,1,0:T(8,128)(2,1)}) custom-call(bf16[128,2048]{1,0:T(8,128)(2,1)} %tokens.1, s32[2,128]{1,0:T(2,128)} %bitcast.2, f32[2,128]{1,0:T(2,128)} %bitcast.3, bf16[4,2048,768]{2,1,0:T(8,128)(2,1)} %w_gate.1, bf16[4,2048,768]{2,1,0:T(8,128)(2,1)} %w_up.1, ...), custom_call_target="tpu_custom_call" | custom-call | flops 9663676416 | bytes 37748736 | tf_op jit(solution)/shard_map/pallas_call | solution.py:468
  40.4 2.0 %shard_map.122 = (bf16[128,2048]{1,0:T(8,128)(2,1)}, f32[96,128]{1,0:T(8,128)}, bf16[1,96,2048]{2,1,0:T(8,128)(2,1)}) custom-call(bf16[128,2048]{1,0:T(8,128)(2,1)} %get-tuple-element.6.moe_in, f32[96,128]{1,0:T(8,128)} %get-tuple-element.7.momentum_in, bf16[1,96,2048]{2,1,0:T(8,128)(2,1)} %get-tuple-element.8.local_in), custom_call_target="tpu_custom_call" | custom-call | tf_op jit(solution)/shard_map/pallas_call | solution.py:538

commit v4 on v3

--- a/solution.py
+++ b/solution.py
@@ -83,6 +83,7 @@
 
 
 LANES = 128
+STRIP = 256
 MESH = pl.DeviceIdType.MESH
 
 
@@ -101,8 +102,7 @@
     moe_out,
     momentum_next,
     local_next,
-    gate_s,
-    up_s,
+    pair_s,
     down_s,
     tok,
     mix_all,
@@ -130,6 +130,7 @@
     upd,
     mom_out,
     loc_out,
+    pair_sem,
     w_sem,
     in_sem,
     out_sem,
@@ -165,14 +166,25 @@
     def columns(index):
         return pl.ds(pl.multiple_of(index * LANES, LANES), LANES)
 
-    weights = []
-    for e in range(experts):
-        weights.append(pltpu.make_async_copy(w_gate.at[e], gate_s.at[e], w_sem.at[0, e]))
-        weights.append(pltpu.make_async_copy(w_up.at[e], up_s.at[e], w_sem.at[1, e]))
-    for e in range(experts):
-        weights.append(
-            pltpu.make_async_copy(w_down.at[e], down_s.at[pl.ds(e * hidden, hidden)], w_sem.at[2, e])
-        )
+    strips = hidden // STRIP
+
+    def pair_copies(e):
+        copies = []
+        for f in range(strips):
+            for side, source in ((0, w_gate), (1, w_up)):
+                copies.append(
+                    pltpu.make_async_copy(
+                        source.at[e, :, pl.ds(f * STRIP, STRIP)],
+                        pair_s.at[e, :, pl.ds((2 * f + side) * STRIP, STRIP)],
+                        pair_sem.at[e, 2 * f + side],
+                    )
+                )
+        return copies
+
+    down_copies = [
+        pltpu.make_async_copy(w_down.at[e], down_s.at[pl.ds(e * hidden, hidden)], w_sem.at[e])
+        for e in range(experts)
+    ]
     load_tok = pltpu.make_async_copy(tokens, tok.at[pl.ds(0, rows)], in_sem.at[0])
     load_glob = pltpu.make_async_copy(global_params, glob_s, in_sem.at[1])
     load_mom = pltpu.make_async_copy(momentum, mom_s, in_sem.at[2])
@@ -186,7 +198,7 @@
 
     load_mom.start()
     load_tok.start()
-    for copy in weights[:2]:
+    for copy in pair_copies(0):
         copy.start()
     for copy in load_grad:
         copy.start()
@@ -236,7 +248,10 @@
     for j in range(1, chips):
         send_mom.append(remote(upd.at[rep, 0], upd.at[rep, 0], mom_sem, (j - 1,), peer(j)))
         send_mom[j - 1].start()
-    for copy in weights[2:]:
+    for e in range(1, experts):
+        for copy in pair_copies(e):
+            copy.start()
+    for copy in down_copies:
         copy.start()
     load_loc.start()
     load_glob.start()
@@ -247,15 +262,17 @@
         chosen = jnp.where(lanes == shard * experts + e, mix_all[part, :], 0.0)
         scale = jnp.sum(chosen, axis=1, keepdims=True)
         tok_part = tok[part, :]
-        for f in range(0, hidden, 256):
-            gate = jnp.dot(tok_part, gate_s[e, :, f : f + 256], preferred_element_type=jnp.float32)
-            upward = jnp.dot(tok_part, up_s[e, :, f : f + 256], preferred_element_type=jnp.float32)
+        for f in range(strips):
+            both = pair_s[e, :, 2 * f * STRIP : 2 * (f + 1) * STRIP]
+            pair = jnp.dot(tok_part, both, preferred_element_type=jnp.float32)
+            gate, upward = pair[:, :STRIP], pair[:, STRIP:]
             value = gate / (1.0 + jnp.exp(-gate)) * upward * scale
-            hid[part, pl.ds(pl.multiple_of(e * hidden + f, LANES), 256)] = value.astype(jnp.bfloat16)
+            place = pl.ds(pl.multiple_of(e * hidden + f * STRIP, STRIP), STRIP)
+            hid[part, place] = value.astype(jnp.bfloat16)
 
     def weights_in(e):
-        pltpu.make_async_copy(w_gate.at[e], gate_s.at[e], w_sem.at[0, e]).wait()
-        pltpu.make_async_copy(w_up.at[e], up_s.at[e], w_sem.at[1, e]).wait()
+        for copy in pair_copies(e):
+            copy.wait()
 
     def steps(start, count, first, last, fresh):
         def one(e, carry):
@@ -294,7 +311,7 @@
     send_tok[0].wait_recv()
     steps(rows, chunk_rows, 0, early, False)
     steps(0, rows + chunk_rows, early, experts, True)
-    for copy in weights[2 * experts :]:
+    for copy in down_copies:
         copy.wait()
 
     def down(start, count, t):
@@ -471,8 +488,7 @@
         in_specs=[anywhere, in_vmem, in_vmem] + [anywhere] * 7,
         out_specs=(anywhere,) * 3,
         scratch_shapes=[
-            pltpu.VMEM(w_gate.shape, bf16),
-            pltpu.VMEM(w_up.shape, bf16),
+            pltpu.VMEM((experts, width, 2 * hidden), bf16),
             pltpu.VMEM((experts * hidden, width), bf16),
             pltpu.VMEM((2 * rows, width), bf16),
             pltpu.VMEM((2 * rows, LANES), f32),
@@ -500,7 +516,8 @@
             pltpu.VMEM((reps, 2) + block, bf16),
             pltpu.VMEM(block, f32),
             pltpu.VMEM((frag_rows, width), bf16),
-            dma((3, experts)),
+            dma((experts, 2 * hidden // STRIP)),
+            dma((experts,)),
             dma((4,)),
             dma((2 + chunks,)),
             dma((chips,)),

time: 42.6 us -> 42.7 us (level)
  no operation moved by 1% of the time
where the time goes in v4:
time: 42.7 us; the launch traced here: 42.5 us
  Pallas kernels  41.9 us (98%)
  between operations  0.64 us (1%)
    pallas_call x1, Pallas kernels, fused(): pl.pallas_call(functools.partial(kernel, reps), out_shape=out_shape, in_s...  39.9 us
    pallas_call x1, Pallas kernels, fused(): pl.pallas_call(closing, out_shape=out_shape, in_specs=[anywhere] * 3, out...  1.98 us

profile of v4, /device:TPU:0, one launch (start us, length us, event | category | flops | bytes accessed | tf_op | source)
XLA Modules:
  0.0 42.5 jit_solution(8300572469298569746)
XLA Ops:
  0.6 39.9 %shard_map.121 = (bf16[128,2048]{1,0:T(8,128)(2,1)}, f32[96,128]{1,0:T(8,128)}, bf16[1,96,2048]{2,1,0:T(8,128)(2,1)}) custom-call(bf16[128,2048]{1,0:T(8,128)(2,1)} %tokens.1, s32[2,128]{1,0:T(2,128)} %bitcast.2, f32[2,128]{1,0:T(2,128)} %bitcast.3, bf16[4,2048,768]{2,1,0:T(8,128)(2,1)} %w_gate.1, bf16[4,2048,768]{2,1,0:T(8,128)(2,1)} %w_up.1, ...), custom_call_target="tpu_custom_call" | custom-call | flops 9663676416 | bytes 37748736 | tf_op jit(solution)/shard_map/pallas_call | solution.py:485
  40.6 2.0 %shard_map.122 = (bf16[128,2048]{1,0:T(8,128)(2,1)}, f32[96,128]{1,0:T(8,128)}, bf16[1,96,2048]{2,1,0:T(8,128)(2,1)}) custom-call(bf16[128,2048]{1,0:T(8,128)(2,1)} %get-tuple-element.6.moe_in, f32[96,128]{1,0:T(8,128)} %get-tuple-element.7.momentum_in, bf16[1,96,2048]{2,1,0:T(8,128)(2,1)} %get-tuple-element.8.local_in), custom_call_target="tpu_custom_call" | custom-call | tf_op jit(solution)/shard_map/pallas_call | solution.py:555

commit v5 on v4

--- a/solution.py
+++ b/solution.py
@@ -116,6 +116,7 @@
     grad_own,
     grad_sib,
     grad_sum,
+    grad_half,
     grad_far,
     sq_own,
     sq_far,
@@ -144,6 +145,7 @@
     one_sem,
     mom_sem,
     upd_sem,
+    side_sem,
     fwd_sem,
 ):
     experts = w_gate.shape[0]
@@ -245,9 +247,10 @@
     load_mom.wait()
     upd[rep, 0] = mom_s[...].astype(jnp.bfloat16)
     send_mom = []
-    for j in range(1, chips):
-        send_mom.append(remote(upd.at[rep, 0], upd.at[rep, 0], mom_sem, (j - 1,), peer(j)))
-        send_mom[j - 1].start()
+    along = range(2, chips, 2)
+    for k, j in enumerate(along):
+        send_mom.append(remote(upd.at[rep, 0], upd.at[rep, 0], mom_sem, (k,), peer(j)))
+        send_mom[k].start()
     for e in range(1, experts):
         for copy in pair_copies(e):
             copy.start()
@@ -293,14 +296,16 @@
         copy.wait_recv()
 
     def chip_sum(k, carry):
-        grad_sum[k] = grad_own[k] + grad_sib[k]
+        both_cores = grad_own[k] + grad_sib[k]
+        grad_sum[k] = both_cores
+        grad_half[k] = both_cores.astype(jnp.bfloat16)
         return carry
 
     lax.fori_loop(0, chips, chip_sum, 0)
     send_far = []
     for j in range(1, chips):
         send_far.append(
-            remote(grad_sum.at[(chip + j) % chips], grad_far.at[j - 1], far_sem, (j - 1,), peer(j))
+            remote(grad_half.at[(chip + j) % chips], grad_far.at[j - 1], far_sem, (j - 1,), peer(j))
         )
         send_far[j - 1].start()
 
@@ -338,7 +343,7 @@
         copy.wait_recv()
     total = grad_sum[chip]
     for j in range(1, chips):
-        total = total + grad_far[j - 1]
+        total = total + grad_far[j - 1].astype(jnp.float32)
     mean = total / reps
     squares = mean * mean
     square = squares[0:8]
@@ -348,11 +353,23 @@
     mean_s[...] = mean
     upd[rep, 1] = mean.astype(jnp.bfloat16)
     send_upd = []
-    for j in range(1, chips):
-        send_upd.append(remote(upd.at[rep, 1], upd.at[rep, 1], upd_sem, (j - 1,), peer(j)))
-        send_upd[j - 1].start()
-    forward = [remote(upd.at[rep], upd.at[rep], fwd_sem, (0,), sibling)]
-    forward[0].start()
+    for k, j in enumerate(along):
+        send_upd.append(remote(upd.at[rep, 1], upd.at[rep, 1], upd_sem, (k,), peer(j)))
+        send_upd[k].start()
+    side = chip + 1 - 2 * (chip % 2)
+    origins, across, forward = [], [], []
+
+    def pass_on(origin, further):
+        came = origin * 2 + core
+        if further:
+            device = (side * 2 + core, shard)
+            across.append(remote(upd.at[came], upd.at[came], side_sem, (len(across),), device))
+            across[-1].start()
+        forward.append(remote(upd.at[came], upd.at[came], fwd_sem, (len(forward),), sibling))
+        forward[-1].start()
+        origins.append(origin)
+
+    pass_on(chip, True)
     send_sq = []
     for j in range(1, chips):
         send_sq.append(remote(sq_own, sq_far.at[j - 1], sq_sem, (j - 1,), peer(j)))
@@ -374,13 +391,14 @@
     to_other.start()
     for t in range(tiles):
         give_back(1, t, down(rows + chunk_rows, chunk_rows, t))
-
-    for j in range(1, chips):
-        send_mom[j - 1].wait_recv()
-        send_upd[j - 1].wait_recv()
-        came = ((chip - j + chips) % chips) * 2 + core
-        forward.append(remote(upd.at[came], upd.at[came], fwd_sem, (j,), sibling))
-        forward[j].start()
+        if t == tiles // 2 - 1:
+            for k, j in enumerate(along):
+                send_mom[k].wait_recv()
+                send_upd[k].wait_recv()
+                pass_on((chip - j + chips) % chips, True)
+    for k in range(chips // 2):
+        across[k].wait_recv()
+        pass_on((side - 2 * k + chips) % chips, False)
 
     stores = []
 
@@ -416,11 +434,11 @@
         merged = merge_weight * loc_s[:, cols].astype(jnp.float32) + (1.0 - merge_weight) * later
         loc_out[:, cols] = merged.astype(jnp.bfloat16)
 
-    for j in range(chips):
-        merge(((chip - j + chips) % chips) * 2 + core)
-    for j in range(chips):
-        forward[j].wait_recv()
-        merge(((chip - j + chips) % chips) * 2 + 1 - core)
+    for origin in origins:
+        merge(origin * 2 + core)
+    for copy, origin in zip(forward, origins):
+        copy.wait_recv()
+        merge(origin * 2 + 1 - core)
     store_loc = pltpu.make_async_copy(loc_out, local_next.at[0], out_sem.at[1])
     store_loc.start()
 
@@ -428,7 +446,7 @@
 
     for copy in [send_mix, to_sib, to_other] + send_tok + send_sib + send_far + send_sq + send_back:
         copy.wait_send()
-    for copy in send_mom + send_upd + forward:
+    for copy in send_mom + send_upd + across + forward:
         copy.wait_send()
     for copy in stores + [store_mom, store_loc]:
         copy.wait()
@@ -502,7 +520,8 @@
             pltpu.VMEM((chips,) + block, f32),
             pltpu.VMEM((chips,) + block, f32),
             pltpu.VMEM((chips,) + block, f32),
-            pltpu.VMEM((chips - 1,) + block, f32),
+            pltpu.VMEM((chips,) + block, bf16),
+            pltpu.VMEM((chips - 1,) + block, bf16),
             pltpu.VMEM((8, LANES), f32),
             pltpu.VMEM((chips - 1, 8, LANES), f32),
             pltpu.VMEM((8, LANES), f32),
@@ -530,6 +549,7 @@
             dma((2, 2)),
             dma((2, chips - 1)),
             dma((2, chips - 1)),
+            dma((2, chips // 2)),
             dma((2, chips)),
         ],
         compiler_params=pltpu.CompilerParams(
@@ -585,7 +605,7 @@
 
     def step(*arrays):
         tokens, w_gate, momentum = arrays[0], arrays[3], arrays[8]
-        pairs = shards == 2 and reps % 2 == 0 and reps >= 4
+        pairs = shards == 2 and reps % 4 == 0 and reps >= 8
         aligned = momentum.shape[1] == LANES and tokens.shape[0] == LANES
         if pairs and aligned and w_gate.shape[0] * shards == 8:
             return fused(reps, *arrays)

time: 42.7 us -> 42 us (0.984)
  Pallas kernels: 41.9 us -> 41.2 us
    pallas_call x1, Pallas kernels: 39.9 us -> 39.2 us  [fused(): pl.pallas_call(functools.partial(kernel, reps), out_shape=out_shape, in_s...]
where the time goes in v5:
time: 42 us; the launch traced here: 41.8 us
  Pallas kernels  41.2 us (98%)
  between operations  0.64 us (2%)
    pallas_call x1, Pallas kernels, fused(): pl.pallas_call(functools.partial(kernel, reps), out_shape=out_shape, in_s...  39.2 us
    pallas_call x1, Pallas kernels, fused(): pl.pallas_call(closing, out_shape=out_shape, in_specs=[anywhere] * 3, out...  1.98 us

profile of v5, /device:TPU:0, one launch (start us, length us, event | category | flops | bytes accessed | tf_op | source)
XLA Modules:
  0.0 41.8 jit_solution(15102666313628882431)
XLA Ops:
  0.6 39.2 %shard_map.121 = (bf16[128,2048]{1,0:T(8,128)(2,1)}, f32[96,128]{1,0:T(8,128)}, bf16[1,96,2048]{2,1,0:T(8,128)(2,1)}) custom-call(bf16[128,2048]{1,0:T(8,128)(2,1)} %tokens.1, s32[2,128]{1,0:T(2,128)} %bitcast.2, f32[2,128]{1,0:T(2,128)} %bitcast.3, bf16[4,2048,768]{2,1,0:T(8,128)(2,1)} %w_gate.1, bf16[4,2048,768]{2,1,0:T(8,128)(2,1)} %w_up.1, ...), custom_call_target="tpu_custom_call" | custom-call | flops 9663676416 | bytes 37748736 | tf_op jit(solution)/shard_map/pallas_call | solution.py:503
  39.8 2.0 %shard_map.122 = (bf16[128,2048]{1,0:T(8,128)(2,1)}, f32[96,128]{1,0:T(8,128)}, bf16[1,96,2048]{2,1,0:T(8,128)(2,1)}) custom-call(bf16[128,2048]{1,0:T(8,128)(2,1)} %get-tuple-element.6.moe_in, f32[96,128]{1,0:T(8,128)} %get-tuple-element.7.momentum_in, bf16[1,96,2048]{2,1,0:T(8,128)(2,1)} %get-tuple-element.8.local_in), custom_call_target="tpu_custom_call" | custom-call | tf_op jit(solution)/shard_map/pallas_call | solution.py:575
